TPU v7x, 32 devices: a whole 2x2x4 slice. The times are simulated.
32 devices in a mesh: row: 4 (over x, core), col: 8 (over z, y).
Axes of the slice: x: 2, y: 2, z: 4, core: 2. Of those that a mesh axis runs over, the one named last changes fastest.
Arguments:
- tokens: bfloat16 [128, 8192], P('col', 'row'), may hold values from -6 to 6
- cotangent: bfloat16 [128, 8192], P('col', 'row'), may hold values from -1.5 to 1.5
- gate_weight: bfloat16 [8192, 14336], P('row', 'col'), may hold values from -0.0625 to 0.0625
- up_weight: bfloat16 [8192, 14336], P('row', 'col'), may hold values from -0.0625 to 0.0625
- down_weight: bfloat16 [14336, 8192], P('col', 'row'), may hold values from -0.046875 to 0.046875
Outputs:
- grad_tokens: bfloat16 [128, 8192], P('col', 'row')
- grad_gate: bfloat16 [8192, 14336], P('row', 'col')
- grad_up: bfloat16 [8192, 14336], P('row', 'col')
- grad_down: bfloat16 [14336, 8192], P('col', 'row')
All inputs are finite; a program needn't handle non-finite values.
Results may differ from a plain program's by a relative error of at most 0.0051.
Values may be sent and summed in bfloat16 or wider, within the bound.
A program may use at most 128 MiB of HBM per device.

v0:
```python
import jax
import jax.numpy as jnp
from jax import lax
from jax.sharding import PartitionSpec as P


def contract_last(left, right):
    return lax.dot_general(
        left, right, (((1,), (1,)), ((), ())), preferred_element_type=jnp.float32
    )


def contract_first(left, right):
    return lax.dot_general(
        left, right, (((0,), (0,)), ((), ())), preferred_element_type=jnp.float32
    )


def gating(gate, up, grad_hidden):
    sig = jax.nn.sigmoid(gate)
    act = gate * sig
    hidden = (act * up).astype(jnp.bfloat16)
    d_up = (grad_hidden * act).astype(jnp.bfloat16)
    d_gate = (grad_hidden * up * sig * (1.0 + gate * (1.0 - sig))).astype(jnp.bfloat16)
    return (jnp.concatenate([d_gate, d_up], axis=1), hidden)


def local(tokens, cotangent, gate_weight, up_weight, down_weight):
    tok_all, cot_all = (
        lax.all_gather(tokens, "col", axis=0, tiled=True),
        lax.all_gather(cotangent, "col", axis=0, tiled=True),
    )
    width = gate_weight.shape[1]
    both_weights = jnp.concatenate([gate_weight, up_weight], axis=1)
    piece = tok_all
    summed = lax.psum_scatter(
        jnp.dot(piece, both_weights, preferred_element_type=jnp.float32),
        "row",
        scatter_dimension=0,
        tiled=True,
    )
    piece = cot_all
    grad_hidden = lax.psum_scatter(
        contract_last(piece, down_weight), "row", scatter_dimension=0, tiled=True
    )
    paired, hidden = gating(summed[:, :width], summed[:, width:], grad_hidden)
    paired_all, hidden_all = (
        lax.all_gather(paired, "row", axis=0, tiled=True),
        lax.all_gather(hidden, "row", axis=0, tiled=True),
    )
    grad_both = contract_first(tok_all, paired_all)
    grad_gate = grad_both[:, :width].astype(jnp.bfloat16)
    grad_up = grad_both[:, width:].astype(jnp.bfloat16)
    grad_down = contract_first(hidden_all, cot_all).astype(jnp.bfloat16)
    piece = paired_all
    grad_tokens = lax.psum_scatter(
        contract_last(piece, both_weights), "col", scatter_dimension=0, tiled=True
    ).astype(jnp.bfloat16)
    return (grad_tokens, grad_gate, grad_up, grad_down)


def solution(mesh):
    return jax.shard_map(
        local,
        mesh=mesh,
        in_specs=(
            P("col", "row"),
            P("col", "row"),
            P("row", "col"),
            P("row", "col"),
            P("col", "row"),
        ),
        out_specs=(P("col", "row"), P("row", "col"), P("row", "col"), P("col", "row")),
        check_vma=False,
    )
```

profile of v0, /device:TPU:0, one launch (start us, length us, event | category | flops | bytes accessed | tf_op | source)
XLA Modules:
  0.0 231.6 jit_solution(5471020805838805017)
XLA Ops:
  7.2 0.0 reduce-scatter.4.cloned.1.call-start
  7.2 33.2 %all_gather.12 = bf16[128,2048]{1,0:T(8,128)(2,1)S(1)} all-gather(bf16[16,2048]{1,0:T(8,128)(2,1)} %param.6), channel_id=1, replica_groups=mesh['row'=4,'col'=8] {'col'}, dimensions={0}, use_global_device_ids=true | all-gather | bytes 589824 | tf_op jit(solution)/shard_map/all_gather | solution.py:31
  40.4 6.5 %fusion.3 = f32[128,1792]{1,0:T(8,128)} fusion(bf16[128,2048]{1,0:T(8,128)(2,1)S(1)} %all_gather.12, bf16[1792,2048]{1,0:T(8,128)(2,1)} %param.9), kind=kOutput, calls=%fused_computation.13 | convolution fusion | flops 939524096 | bytes 8781824 | tf_op jit(solution)/shard_map/dot_general | solution.py:8
  47.0 0.0 reduce-scatter.4.cloned.1.call-update
  47.0 0.0 reduce-scatter.6.cloned.1.call-start
  47.1 6.6 %constant_dynamic-update-slice_fusion.1 = bf16[2048,3584]{1,0:T(8,128)(2,1)} fusion(bf16[2048,1792]{1,0:T(8,128)(2,1)} %param.7), kind=kLoop, calls=%fused_computation.11 | loop fusion | bytes 14680064
  53.7 31.3 %all_gather.13 = bf16[128,2048]{1,0:T(8,128)(2,1)S(1)} all-gather(bf16[16,2048]{1,0:T(8,128)(2,1)S(1)} %copy-done), channel_id=1, replica_groups=mesh['row'=4,'col'=8] {'col'}, dimensions={0}, use_global_device_ids=true | all-gather | bytes 589824 | tf_op jit(solution)/shard_map/all_gather | solution.py:30
  84.9 6.6 %constant_dynamic-update-slice_fusion = bf16[2048,3584]{1,0:T(8,128)(2,1)} fusion(bf16[2048,3584]{1,0:T(8,128)(2,1)} %constant_dynamic-update-slice_fusion.1, bf16[2048,1792]{1,0:T(8,128)(2,1)} %param.8), kind=kLoop, calls=%fused_computation.10 | loop fusion | bytes 14680064 | tf_op jit(solution)/shard_map/concatenate | solution.py:34
  91.5 8.5 %convolution_bitcast_fusion = f32[128,3584]{1,0:T(8,128)} fusion(bf16[128,2048]{1,0:T(8,128)(2,1)S(1)} %all_gather.13, bf16[2048,3584]{1,0:T(8,128)(2,1)} %constant_dynamic-update-slice_fusion), kind=kOutput, calls=%fused_computation.3 | convolution fusion | flops 1879048192 | bytes 17039360 | tf_op jit(solution)/shard_map/dot_general | solution.py:37
  100.0 0.0 reduce-scatter.6.cloned.1.call-update
  100.0 0.0 reduce-scatter.8.cloned.1.call-start
  100.1 0.0 reduce-scatter.4.cloned.1.call-done
  100.1 31.1 %reduce-scatter.6.cloned.1.call-done = f32[32,3584]{1,0:T(8,128)} async-done(((f32[128,3584]{1,0:T(8,128)}), f32[32,3584]{1,0:T(8,128)}) %reduce-scatter.6.cloned.1.call-update) | async-done | bytes 458768 | tf_op jit(solution)/shard_map/reduce_scatter | solution.py:36
  131.2 1.3 multiply_convert_fusion.2
  132.5 8.9 %all_gather.14 = bf16[128,3584]{1,0:T(8,128)(2,1)S(1)} all-gather(bf16[32,3584]{1,0:T(8,128)(2,1)S(1)} %pad_maximum_fusion), channel_id=1, replica_groups=mesh['row'=4,'col'=8] {'row'}, dimensions={0}, use_global_device_ids=true | all-gather | bytes 1146880 | tf_op jit(solution)/shard_map/all_gather | solution.py:48
  141.4 10.9 %fusion.4 = f32[128,2048]{1,0:T(8,128)} fusion(bf16[128,3584]{1,0:T(8,128)(2,1)S(1)} %all_gather.14, bf16[2048,3584]{1,0:T(8,128)(2,1)} %constant_dynamic-update-slice_fusion), kind=kOutput, calls=%fused_computation.14 | convolution fusion | flops 1879048192 | bytes 16646144 | tf_op jit(solution)/shard_map/dot_general | solution.py:8
  152.3 7.3 %fusion = bf16[2048,3584]{0,1:T(8,128)(2,1)} fusion(bf16[128,3584]{1,0:T(8,128)(2,1)S(1)} %all_gather.14, bf16[128,2048]{1,0:T(8,128)(2,1)S(1)} %all_gather.13), kind=kOutput, calls=%fused_computation.1 | convolution fusion | flops 1886388224 | bytes 16121856 | tf_op jit(solution)/shard_map/dot_general | solution.py:14
  159.6 10.8 %fusion.2 = (bf16[2048,1792]{0,1:T(8,128)(2,1)}, bf16[2048,1792]{0,1:T(8,128)(2,1)}) fusion(bf16[2048,3584]{0,1:T(8,128)(2,1)} %fusion), kind=kLoop, calls=%fused_computation.12 | loop fusion | bytes 29360128 | tf_op jit(solution)/shard_map/slice | solution.py:53
  170.5 10.0 %copy.10 = bf16[2048,1792]{1,0:T(8,128)(2,1)} copy(bf16[2048,1792]{0,1:T(8,128)(2,1)} %get-tuple-element.9) | data formatting | bytes 14680064
  180.4 9.9 %copy.11 = bf16[2048,1792]{1,0:T(8,128)(2,1)} copy(bf16[2048,1792]{0,1:T(8,128)(2,1)} %get-tuple-element.8) | data formatting | bytes 14680064
  190.4 7.0 %all_gather.15 = bf16[128,1792]{1,0:T(8,128)(2,1)S(1)} all-gather(bf16[32,1792]{1,0:T(8,128)(2,1)S(1)} %get-tuple-element.12), channel_id=1, replica_groups=mesh['row'=4,'col'=8] {'row'}, dimensions={0}, use_global_device_ids=true | all-gather | bytes 573440 | tf_op jit(solution)/shard_map/all_gather | solution.py:49
  197.4 5.1 %convolution_convert_fusion.1 = bf16[1792,2048]{1,0:T(8,128)(2,1)} fusion(bf16[128,1792]{1,0:T(8,128)(2,1)S(1)} %all_gather.15, bf16[128,2048]{1,0:T(8,128)(2,1)S(1)} %all_gather.12), kind=kOutput, calls=%fused_computation.2 | convolution fusion | flops 943194112 | bytes 8323072 | tf_op jit(solution)/shard_map/dot_general | solution.py:14
  202.5 21.0 %reduce-scatter.8.cloned.1.call-done = f32[16,2048]{1,0:T(8,128)} async-done(((f32[128,2048]{1,0:T(8,128)}), f32[16,2048]{1,0:T(8,128)}) %reduce-scatter.8.cloned.1.call-update) | async-done | bytes 131088 | tf_op jit(solution)/shard_map/reduce_scatter | solution.py:56
  223.5 1.5 convert_element_type.19
  (4 shorter events, 0.0 us)
Async XLA Ops:
  7.2 92.9 %reduce-scatter.4.cloned.1.call-start = ((), (), s32[]{:S(2)}) async-start(), calls=%async_computation.3 | async-start | bytes 1146880 | tf_op jit(solution)/shard_map/reduce_scatter | solution.py:43
  47.0 6.7 %copy-start = (bf16[16,2048]{1,0:T(8,128)(2,1)S(1)}, bf16[16,2048]{1,0:T(8,128)(2,1)}, u32[]{:S(2)}) copy-start(bf16[16,2048]{1,0:T(8,128)(2,1)} %param.5) | copy-start | bytes 196612
  47.0 84.2 %reduce-scatter.6.cloned.1.call-start = ((), (), s32[]{:S(2)}) async-start(), calls=%async_computation.4 | async-start | bytes 2293760 | tf_op jit(solution)/shard_map/reduce_scatter | solution.py:36
  100.0 123.5 %reduce-scatter.8.cloned.1.call-start = ((), (), s32[]{:S(2)}) async-start(), calls=%async_computation.5 | async-start | bytes 1179648 | tf_op jit(solution)/shard_map/reduce_scatter | solution.py:56
Sparse Core Ops, SparseCore 0:
  47.1 25.1 reduce-scatter.3
  100.1 30.9 reduce-scatter.5
  159.7 63.7 reduce-scatter.7
where the time goes:
time: 232 us
  blocking collectives  80.4 us (35%)
  waiting for transfers between devices  52.1 us (22%)
  local copies, waits for them, and re-layouts  43.9 us (19%)
  matrix products  38.4 us (17%)
  between operations  13.8 us (6%)
  other arithmetic  2.84 us (1%)
    all_gather x1, blocking collectives, local(): lax.all_gather(cotangent, 'col', axis=0, tiled=True)  33.2 us
    all_gather x1, blocking collectives, local(): lax.all_gather(tokens, 'col', axis=0, tiled=True)  31.3 us
    reduce_scatter x1, waiting for transfers between devices, local(): lax.psum_scatter(jnp.dot(piece, both_weights, preferred_element_type=jnp....  31.1 us
    unnamed x5, local copies, waits for them, and re-layouts  26.5 us
    reduce_scatter x1, waiting for transfers between devices, local(): lax.psum_scatter(contract_last(piece, both_weights), 'col', scatter_dimen...  21 us
    dot_general x2, matrix products, contract_last(): lax.dot_general(left, right, (((1,), (1,)), ((), ())), preferred_element_...  17.4 us
    dot_general x2, matrix products, contract_first(): lax.dot_general(left, right, (((0,), (0,)), ((), ())), preferred_element_...  12.4 us
    slice x1, local copies, waits for them, and re-layouts, local(): grad_up = grad_both[:, width:].astype(jnp.bfloat16)  10.8 us
  transfers between devices with their start and end apart: 3, of which 2 were waited for; matrix products, arithmetic and copies ran while one was open for 25% of the time, Pallas kernels for 0%

commit v1 on v0

v1 whole, which is shorter than its diff:
```python
import functools

import jax
import jax.numpy as jnp
from jax import lax
from jax.experimental import pallas as pl
from jax.experimental.pallas import tpu as pltpu
from jax.sharding import PartitionSpec as P

MESH = pl.DeviceIdType.MESH
F32, BF16 = jnp.float32, jnp.bfloat16
TILE = 256
GROUPS = 4


def contract_last(left, right):
    return lax.dot_general(
        left, right, (((1,), (1,)), ((), ())), preferred_element_type=F32
    )


def contract_first(left, right):
    return lax.dot_general(
        left, right, (((0,), (0,)), ((), ())), preferred_element_type=F32
    )


def main_kernel(
    tok_ref, cot_ref, wg_hbm, wu_hbm, wd_hbm,
    gt_ref, tok_out, cot_out, dg_out, du_out, hid_out,
    tok_all, cot_all, wg, wu, wd,
    own, core_send, core_recv, x_send, x_recv,
    dg, du, hid,
    part, y_send, y_recv, z_send, z_recv, mine,
    w_sem, out_sem, a_send, a_recv, c_ssem, c_rsem, x_ssem, x_rsem,
    h_ssem, h_rsem, y_ssem, y_rsem, z_ssem, z_rsem,
):
    row, col = lax.axis_index("row"), lax.axis_index("col")
    core, zy = lax.rem(row, 2), lax.rem(col, 2)
    sib = row + 1 - 2 * core
    across = lax.rem(row + 2, 4)
    y_peer = col + 1 - 2 * zy
    z = col // 2
    z_to = [None] + [lax.rem(col + 2 * d, 8) for d in (1, 2, 3)]
    z_from = [None] + [lax.rem(col + 8 - 2 * d, 8) for d in (1, 2, 3)]
    y_from = [None] + [lax.rem(y_peer + 8 - 2 * d, 8) for d in (1, 2, 3)]

    w_copies = [
        pltpu.make_async_copy(src, dst, w_sem.at[k])
        for k, (src, dst) in enumerate(((wg_hbm, wg), (wu_hbm, wu), (wd_hbm, wd)))
    ]
    for copy in w_copies:
        copy.start()

    barrier = pltpu.get_barrier_semaphore()
    for peer in ((sib, col), (across, col), (row, y_peer),
                 (row, z_to[1]), (row, z_to[2]), (row, z_to[3])):
        pl.semaphore_signal(barrier, inc=1, device_id=peer, device_id_type=MESH)
    pl.semaphore_wait(barrier, 6)

    def send(src, dst, ssem, rsem, peer):
        return pltpu.make_async_remote_copy(
            src_ref=src, dst_ref=dst, send_sem=ssem, recv_sem=rsem,
            device_id=peer, device_id_type=MESH,
        )

    n = tok_ref.shape[0]

    def block(index):
        return pl.ds(pl.multiple_of(index * n, n), n)

    gathers = ((tok_ref, tok_all), (cot_ref, cot_all))
    sends = []
    for a, (src, dst) in enumerate(gathers):
        for k, peer in ((2, z_to[2]), (1, z_to[1]), (3, z_to[3]), (0, y_peer)):
            sends.append(send(src, dst.at[block(col)], a_send.at[a, k], a_recv.at[a, k], (row, peer)))
            sends[-1].start()

    def arrived(a, k, source):
        dst = gathers[a][1].at[block(source)]
        send(dst, dst, a_send.at[a, k], a_recv.at[a, k], (row, y_peer)).wait_recv()

    def gather(a):
        src, dst = gathers[a]
        dst[block(col), :] = src[...]
        for d in (1, 3, 2):
            arrived(a, d, z_from[d])
            there = dst.at[block(z_from[d])]
            sends.append(send(there, there, a_send.at[a, 3 + d], a_recv.at[a, 3 + d], (row, y_peer)))
            sends[-1].start()
        arrived(a, 0, y_peer)
        for d in (1, 3, 2):
            arrived(a, 3 + d, y_from[d])

    width = wg.shape[1]
    half = tok_all.shape[0] // 2
    mine_rows = pl.ds(pl.multiple_of(core * half, half), half)

    def split(m, at, full):
        low, high = full[:half], full[half:]
        first = core == 0
        own[m, :, at] = jnp.where(first, low, high)
        core_send[m, :, at] = jnp.where(first, high, low)

    def forward(m):
        @pl.loop(0, width // TILE)
        def _(t):
            at = pl.ds(pl.multiple_of(t * TILE, TILE), TILE)
            if m == 2:
                full = contract_last(cot_all[...], wd[at, :])
            else:
                full = jnp.dot(tok_all[...], (wg, wu)[m][:, at], preferred_element_type=F32)
            split(m, at, full)

    c_copies = [send(core_send.at[m], core_recv.at[m], c_ssem.at[m], c_rsem.at[m], (sib, col)) for m in range(3)]
    x_copies = [send(x_send.at[m], x_recv.at[m], x_ssem.at[m], x_rsem.at[m], (across, col)) for m in range(3)]

    def over_chip(m):
        c_copies[m].wait_recv()

        @pl.loop(0, width // TILE)
        def _(t):
            at = pl.ds(pl.multiple_of(t * TILE, TILE), TILE)
            total = own[m, :, at] + core_recv[m, :, at]
            own[m, :, at] = total
            x_send[m, :, at] = total.astype(BF16)
        x_copies[m].start()

    gather(0)
    for m in range(3):
        if m == 2:
            gather(1)
        w_copies[m].wait()
        forward(m)
        c_copies[m].start()
        if m > 0:
            over_chip(m - 1)
    over_chip(2)

    outs = [
        pltpu.make_async_copy(src, dst, out_sem.at[k])
        for k, (src, dst) in enumerate(
            ((tok_all, tok_out), (cot_all, cot_out), (dg, dg_out), (du, du_out), (hid, hid_out)))
    ]
    outs[0].start()
    outs[1].start()

    for m in range(3):
        x_copies[m].wait_recv()

    @pl.loop(0, width // TILE)
    def _(t):
        at = pl.ds(pl.multiple_of(t * TILE, TILE), TILE)
        gate, up, grad_hidden = (own[m, :, at] + x_recv[m, :, at].astype(F32) for m in range(3))
        sig = jax.nn.sigmoid(gate)
        act = gate * sig
        hid[mine_rows, at] = (act * up).astype(BF16)
        du[mine_rows, at] = (grad_hidden * act).astype(BF16)
        dg[mine_rows, at] = (grad_hidden * up * sig * (1.0 + gate * (1.0 - sig))).astype(BF16)

    h_copies = [
        send(ref.at[mine_rows], ref.at[mine_rows], h_ssem.at[k], h_rsem.at[k], (sib, col))
        for k, ref in enumerate((dg, du, hid))
    ]
    for copy in h_copies:
        copy.start()
    their_rows = pl.ds(pl.multiple_of((1 - core) * half, half), half)
    for k, ref in enumerate((dg, du, hid)):
        there = ref.at[their_rows]
        send(there, there, h_ssem.at[k], h_rsem.at[k], (sib, col)).wait_recv()
    for k in (2, 3, 4):
        outs[k].start()

    span = wg.shape[0] // GROUPS
    y_copies = [send(y_send.at[g], y_recv.at[g], y_ssem.at[g], y_rsem.at[g], (row, y_peer)) for g in range(GROUPS)]
    z_copies = [
        [send(z_send.at[g, d - 1], z_recv.at[g, d - 1], z_ssem.at[g, d - 1], z_rsem.at[g, d - 1], (row, z_to[d]))
         for d in (1, 2, 3)]
        for g in range(GROUPS)
    ]

    def backward(g):
        @pl.loop(0, span // TILE)
        def _(t):
            at = pl.ds(pl.multiple_of(t * TILE, TILE), TILE)
            rows = pl.ds(pl.multiple_of(g * span + t * TILE, TILE), TILE)
            full = contract_last(dg[...], wg[rows, :]) + contract_last(du[...], wu[rows, :])
            part[g, :, :, at] = full.reshape(8, n, TILE)
        for k in range(4):
            y_send[g, k] = part[g, y_peer - 2 * z + 2 * k].astype(BF16)
        y_copies[g].start()

    def along_z(g):
        y_copies[g].wait_recv()
        for d in (1, 2, 3):
            to = lax.rem(z + d, 4)
            z_send[g, d - 1] = (part[g, 2 * to + zy] + y_recv[g, to].astype(F32)).astype(BF16)
            z_copies[g][d - 1].start()
        mine[g] = part[g, col] + y_recv[g, z].astype(F32)

    for g in range(GROUPS):
        backward(g)
        if g > 0:
            along_z(g - 1)
    along_z(GROUPS - 1)
    for g in range(GROUPS):
        total = mine[g]
        for d in (1, 2, 3):
            z_copies[g][d - 1].wait_recv()
            total = total + z_recv[g, d - 1].astype(F32)
        gt_ref[:, g * span:(g + 1) * span] = total.astype(BF16)

    for copy in sends + c_copies + x_copies + h_copies + y_copies:
        copy.wait_send()
    for group in z_copies:
        for copy in group:
            copy.wait_send()
    for copy in outs:
        copy.wait()


def main(tokens, cotangent, gate_weight, up_weight, down_weight):
    n, depth = tokens.shape
    width = gate_weight.shape[1]
    all_tokens = 8 * n
    half = all_tokens // 2
    span = depth // GROUPS
    hbm, vmem = pl.BlockSpec(memory_space=pl.ANY), pl.BlockSpec(memory_space=pltpu.VMEM)
    dma = pltpu.SemaphoreType.DMA
    return pl.pallas_call(
        main_kernel,
        out_shape=(
            jax.ShapeDtypeStruct((n, depth), BF16),
            jax.ShapeDtypeStruct((all_tokens, depth), BF16),
            jax.ShapeDtypeStruct((all_tokens, depth), BF16),
            jax.ShapeDtypeStruct((all_tokens, width), BF16),
            jax.ShapeDtypeStruct((all_tokens, width), BF16),
            jax.ShapeDtypeStruct((all_tokens, width), BF16),
        ),
        in_specs=[vmem, vmem, hbm, hbm, hbm],
        out_specs=(vmem, hbm, hbm, hbm, hbm, hbm),
        scratch_shapes=[
            pltpu.VMEM((all_tokens, depth), BF16),
            pltpu.VMEM((all_tokens, depth), BF16),
            pltpu.VMEM((depth, width), BF16),
            pltpu.VMEM((depth, width), BF16),
            pltpu.VMEM((width, depth), BF16),
            pltpu.VMEM((3, half, width), F32),
            pltpu.VMEM((3, half, width), F32),
            pltpu.VMEM((3, half, width), F32),
            pltpu.VMEM((3, half, width), BF16),
            pltpu.VMEM((3, half, width), BF16),
            pltpu.VMEM((all_tokens, width), BF16),
            pltpu.VMEM((all_tokens, width), BF16),
            pltpu.VMEM((all_tokens, width), BF16),
            pltpu.VMEM((GROUPS, 8, n, span), F32),
            pltpu.VMEM((GROUPS, 4, n, span), BF16),
            pltpu.VMEM((GROUPS, 4, n, span), BF16),
            pltpu.VMEM((GROUPS, 3, n, span), BF16),
            pltpu.VMEM((GROUPS, 3, n, span), BF16),
            pltpu.VMEM((GROUPS, n, span), F32),
            dma((3,)), dma((5,)), dma((2, 7)), dma((2, 7)),
            dma((3,)), dma((3,)), dma((3,)), dma((3,)),
            dma((3,)), dma((3,)), dma((GROUPS,)), dma((GROUPS,)),
            dma((GROUPS, 3)), dma((GROUPS, 3)),
        ],
        compiler_params=pltpu.CompilerParams(
            collective_id=0, has_side_effects=True, vmem_limit_bytes=56 * 1024 * 1024
        ),
    )(tokens, cotangent, gate_weight, up_weight, down_weight)


def weight_kernel(last, tok_ref, dg_ref, du_ref, hid_ref, cot_ref, gg_ref, gu_ref, gd_ref):
    tok = tok_ref[...]
    gg_ref[...] = contract_first(tok, dg_ref[...]).astype(BF16)
    gu_ref[...] = contract_first(tok, du_ref[...]).astype(BF16)

    @pl.when(pl.program_id(0) <= last)
    def _():
        gd_ref[...] = contract_first(hid_ref[...], cot_ref[...]).astype(BF16)


def weight_grads(tok_all, dg, du, hid, cot_all):
    rows, depth = tok_all.shape
    width = dg.shape[1]
    last = width // TILE - 1

    def whole(array):
        return pl.BlockSpec(array.shape, lambda i: (0, 0))

    return pl.pallas_call(
        functools.partial(weight_kernel, last),
        grid=(depth // TILE,),
        out_shape=(
            jax.ShapeDtypeStruct((depth, width), BF16),
            jax.ShapeDtypeStruct((depth, width), BF16),
            jax.ShapeDtypeStruct((width, depth), BF16),
        ),
        in_specs=[
            pl.BlockSpec((rows, TILE), lambda i: (0, i)),
            whole(dg),
            whole(du),
            pl.BlockSpec((rows, TILE), lambda i: (0, jnp.minimum(i, last))),
            whole(cot_all),
        ],
        out_specs=(
            pl.BlockSpec((TILE, width), lambda i: (i, 0)),
            pl.BlockSpec((TILE, width), lambda i: (i, 0)),
            pl.BlockSpec((TILE, depth), lambda i: (jnp.minimum(i, last), 0)),
        ),
        compiler_params=pltpu.CompilerParams(vmem_limit_bytes=40 * 1024 * 1024),
    )(tok_all, dg, du, hid, cot_all)


def local(tokens, cotangent, gate_weight, up_weight, down_weight):
    grad_tokens, tok_all, cot_all, dg, du, hid = main(
        tokens, cotangent, gate_weight, up_weight, down_weight
    )
    grad_gate, grad_up, grad_down = weight_grads(tok_all, dg, du, hid, cot_all)
    return (grad_tokens, grad_gate, grad_up, grad_down)


def gating(gate, up, grad_hidden):
    sig = jax.nn.sigmoid(gate)
    act = gate * sig
    hidden = (act * up).astype(BF16)
    d_up = (grad_hidden * act).astype(BF16)
    d_gate = (grad_hidden * up * sig * (1.0 + gate * (1.0 - sig))).astype(BF16)
    return d_gate, d_up, hidden


def local_any(tokens, cotangent, gate_weight, up_weight, down_weight):
    def gather(array, axis):
        return lax.all_gather(array, axis, axis=0, tiled=True)

    def scatter(array, axis):
        return lax.psum_scatter(array, axis, scatter_dimension=0, tiled=True)

    tok_all, cot_all = gather(tokens, "col"), gather(cotangent, "col")
    gate = scatter(jnp.dot(tok_all, gate_weight, preferred_element_type=F32), "row")
    up = scatter(jnp.dot(tok_all, up_weight, preferred_element_type=F32), "row")
    grad_hidden = scatter(contract_last(cot_all, down_weight), "row")
    dg, du, hid = (gather(part, "row") for part in gating(gate, up, grad_hidden))
    grad_tokens = scatter(
        contract_last(dg, gate_weight) + contract_last(du, up_weight), "col"
    ).astype(BF16)
    return (
        grad_tokens,
        contract_first(tok_all, dg).astype(BF16),
        contract_first(tok_all, du).astype(BF16),
        contract_first(hid, cot_all).astype(BF16),
    )


def solution(mesh):
    fits = mesh.shape["row"] == 4 and mesh.shape["col"] == 8
    return jax.shard_map(
        local if fits else local_any,
        mesh=mesh,
        in_specs=(
            P("col", "row"),
            P("col", "row"),
            P("row", "col"),
            P("row", "col"),
            P("col", "row"),
        ),
        out_specs=(P("col", "row"), P("row", "col"), P("row", "col"), P("col", "row")),
        check_vma=False,
    )
```

time: 232 us -> 81.8 us (0.35)
  blocking collectives: 80.4 us -> 0 us
  Pallas kernels: 0 us -> 74.1 us
  waiting for transfers between devices: 52.1 us -> 0 us
  matrix products: 38.4 us -> 0 us
  local copies, waits for them, and re-layouts: 43.9 us -> 6.6 us
  between operations: 13.8 us -> 0.65 us
  other arithmetic: 2.84 us -> 0 us
    all_gather x4 -> x0, blocking collectives: 80.4 us -> none  [the longest x1 33.2 us: local(): lax.all_gather(cotangent, 'col', axis=0, tiled=True)]
    pallas_call x0 -> x2, Pallas kernels: none -> 74.1 us  [the longest x1 62.8 us: main(): pl.pallas_call(main_kernel, out_shape=(jax.ShapeDtypeStruct((n, depth), B...]
    reduce_scatter x3 -> x0, waiting for transfers between devices: 52.1 us -> none  [the longest x1 31.1 us: local(): lax.psum_scatter(jnp.dot(piece, both_weights, preferred_element_type=jnp....]
    dot_general x5 -> x0, matrix products: 38.4 us -> none  [the longest x2 17.4 us: contract_last(): lax.dot_general(left, right, (((1,), (1,)), ((), ())), preferred_element_...]
    unnamed x5 -> x11, local copies, waits for them, and re-layouts: 26.5 us -> 6.6 us
    slice x1 -> x0, local copies, waits for them, and re-layouts: 10.8 us -> none  [local(): grad_up = grad_both[:, width:].astype(jnp.bfloat16)]
    concatenate x1 -> x0, local copies, waits for them, and re-layouts: 6.56 us -> none  [local(): both_weights = jnp.concatenate([gate_weight, up_weight], axis=1)]
    convert_element_type x2 -> x0, other arithmetic: 2.82 us -> none  [the longest x1 1.54 us: local(): grad_tokens = lax.psum_scatter(contract_last(piece, both_weights), 'col',...]
  transfers between devices with their start and end apart: 3 -> 0, of which waited for: 2 -> 0; matrix products, arithmetic and copies ran while one was open for 25% -> 0% of each run, Pallas kernels for 0% -> 0%
where the time goes in v1:
time: 81.8 us; the launch traced here: 81.4 us
  Pallas kernels  74.1 us (91%)
  local copies, waits for them, and re-layouts  6.6 us (8%)
    pallas_call x1, Pallas kernels, main(): pl.pallas_call(main_kernel, out_shape=(jax.ShapeDtypeStruct((n, depth), B...  62.8 us
    pallas_call x1, Pallas kernels, weight_grads(): pl.pallas_call(functools.partial(weight_kernel, last), grid=(depth // TIL...  11.3 us
    unnamed x11, local copies, waits for them, and re-layouts  6.6 us

profile of v1, /device:TPU:0, one launch (start us, length us, event | category | flops | bytes accessed | tf_op | source)
XLA Modules:
  0.0 81.4 jit_solution(1016923466607173413)
XLA Ops:
  0.6 62.8 %shard_map.84 = (bf16[16,2048]{1,0:T(8,128)(2,1)}, bf16[128,2048]{1,0:T(8,128)(2,1)}, bf16[128,2048]{1,0:T(8,128)(2,1)}, bf16[128,1792]{1,0:T(8,128)(2,1)}, bf16...) custom-call(bf16[16,2048]{1,0:T(8,128)(2,1)} %tok_ref.1, bf16[16,2048]{1,0:T(8,128)(2,1)} %cot_ref.1, ...), custom_call_target="tpu_custom_call" | custom-call | tf_op jit(solution)/shard_map/pallas_call | solution.py:230
  63.4 0.0 copy-start
  63.4 1.0 %copy-done = bf16[128,2048]{1,0:T(8,128)(2,1)S(1)} copy-done((bf16[128,2048]{1,0:T(8,128)(2,1)S(1)}, bf16[128,2048]{1,0:T(8,128)(2,1)}, u32[]{:S(2)}) %copy-start) | copy-done | bytes 524312
  64.5 0.0 copy-start.1
  64.5 1.0 %copy-done.1 = bf16[128,2048]{1,0:T(8,128)(2,1)S(1)} copy-done((bf16[128,2048]{1,0:T(8,128)(2,1)S(1)}, bf16[128,2048]{1,0:T(8,128)(2,1)}, u32[]{:S(2)}) %copy-start.1) | copy-done | bytes 524312
  65.5 0.0 copy-start.2
  65.5 1.0 %copy-done.2 = bf16[128,1792]{1,0:T(8,128)(2,1)S(1)} copy-done((bf16[128,1792]{1,0:T(8,128)(2,1)S(1)}, bf16[128,1792]{1,0:T(8,128)(2,1)}, u32[]{:S(2)}) %copy-start.2) | copy-done | bytes 458776
  66.5 0.0 copy-start.3
  66.5 1.0 %copy-done.3 = bf16[128,1792]{1,0:T(8,128)(2,1)S(1)} copy-done((bf16[128,1792]{1,0:T(8,128)(2,1)S(1)}, bf16[128,1792]{1,0:T(8,128)(2,1)}, u32[]{:S(2)}) %copy-start.3) | copy-done | bytes 458776
  67.5 0.0 copy-start.4
  67.5 1.0 %copy-done.4 = bf16[128,1792]{1,0:T(8,128)(2,1)S(1)} copy-done((bf16[128,1792]{1,0:T(8,128)(2,1)S(1)}, bf16[128,1792]{1,0:T(8,128)(2,1)}, u32[]{:S(2)}) %copy-start.4) | copy-done | bytes 458776
  68.6 11.3 %shard_map.85 = (bf16[2048,1792]{1,0:T(8,128)(2,1)}, bf16[2048,1792]{1,0:T(8,128)(2,1)}, bf16[1792,2048]{1,0:T(8,128)(2,1)}) custom-call(bf16[128,2048]{1,0:T(8,128)(2,1)S(1)} %copy-done, bf16[128,1792]{1,0:T(8,128)(2,1)S(1)} %copy-done.2, bf16[128,1792]{1,0:T(8,128)(2,1)S(1)} %copy-done.3, bf16[128,1792]{1,0:T(8,128)(2,1)S(1)} %copy-done.4, ...), custom_call_target="tpu_custom_call" | custom-call | tf_op jit(solution)/shard_map/pallas_call | solution.py:291
  79.9 1.5 %copy.10 = bf16[16,2048]{1,0:T(8,128)(2,1)} copy(bf16[16,2048]{1,0:T(8,128)(2,1)} %get-tuple-element.26) | data formatting | bytes 131072
Async XLA Ops:
  63.4 1.0 %copy-start = (bf16[128,2048]{1,0:T(8,128)(2,1)S(1)}, bf16[128,2048]{1,0:T(8,128)(2,1)}, u32[]{:S(2)}) copy-start(bf16[128,2048]{1,0:T(8,128)(2,1)} %get-tuple-element.14.tok_ref) | copy-start | bytes 1572868
  64.5 1.0 %copy-start.1 = (bf16[128,2048]{1,0:T(8,128)(2,1)S(1)}, bf16[128,2048]{1,0:T(8,128)(2,1)}, u32[]{:S(2)}) copy-start(bf16[128,2048]{1,0:T(8,128)(2,1)} %get-tuple-element.18.cot_ref) | copy-start | bytes 1572868
  65.5 1.0 %copy-start.2 = (bf16[128,1792]{1,0:T(8,128)(2,1)S(1)}, bf16[128,1792]{1,0:T(8,128)(2,1)}, u32[]{:S(2)}) copy-start(bf16[128,1792]{1,0:T(8,128)(2,1)} %get-tuple-element.15.dg_ref) | copy-start | bytes 1376260
  66.5 1.0 %copy-start.3 = (bf16[128,1792]{1,0:T(8,128)(2,1)S(1)}, bf16[128,1792]{1,0:T(8,128)(2,1)}, u32[]{:S(2)}) copy-start(bf16[128,1792]{1,0:T(8,128)(2,1)} %get-tuple-element.16.du_ref) | copy-start | bytes 1376260
  67.5 1.0 %copy-start.4 = (bf16[128,1792]{1,0:T(8,128)(2,1)S(1)}, bf16[128,1792]{1,0:T(8,128)(2,1)}, u32[]{:S(2)}) copy-start(bf16[128,1792]{1,0:T(8,128)(2,1)} %get-tuple-element.17.hid_ref) | copy-start | bytes 1376260

commit v2 on v1

--- a/solution.py
+++ b/solution.py
@@ -11,6 +11,7 @@
 F32, BF16 = jnp.float32, jnp.bfloat16
 TILE = 256
 GROUPS = 4
+RELAY = 1
 
 
 def contract_last(left, right):
@@ -71,23 +72,27 @@
 
     gathers = ((tok_ref, tok_all), (cot_ref, cot_all))
     sends = []
-    for a, (src, dst) in enumerate(gathers):
+
+    def spread(a):
+        src, dst = gathers[a]
         for k, peer in ((2, z_to[2]), (1, z_to[1]), (3, z_to[3]), (0, y_peer)):
             sends.append(send(src, dst.at[block(col)], a_send.at[a, k], a_recv.at[a, k], (row, peer)))
             sends[-1].start()
+        dst[block(col), :] = src[...]
 
     def arrived(a, k, source):
         dst = gathers[a][1].at[block(source)]
         send(dst, dst, a_send.at[a, k], a_recv.at[a, k], (row, y_peer)).wait_recv()
 
-    def gather(a):
-        src, dst = gathers[a]
-        dst[block(col), :] = src[...]
+    def relay(a):
+        dst = gathers[a][1]
         for d in (1, 3, 2):
             arrived(a, d, z_from[d])
             there = dst.at[block(z_from[d])]
             sends.append(send(there, there, a_send.at[a, 3 + d], a_recv.at[a, 3 + d], (row, y_peer)))
             sends[-1].start()
+
+    def complete(a):
         arrived(a, 0, y_peer)
         for d in (1, 3, 2):
             arrived(a, 3 + d, y_from[d])
@@ -102,8 +107,8 @@
         own[m, :, at] = jnp.where(first, low, high)
         core_send[m, :, at] = jnp.where(first, high, low)
 
-    def forward(m):
-        @pl.loop(0, width // TILE)
+    def forward(m, run):
+        @pl.loop(run.start // TILE, (run.start + run.size) // TILE)
         def _(t):
             at = pl.ds(pl.multiple_of(t * TILE, TILE), TILE)
             if m == 2:
@@ -112,30 +117,40 @@
                 full = jnp.dot(tok_all[...], (wg, wu)[m][:, at], preferred_element_type=F32)
             split(m, at, full)
 
-    c_copies = [send(core_send.at[m], core_recv.at[m], c_ssem.at[m], c_rsem.at[m], (sib, col)) for m in range(3)]
-    x_copies = [send(x_send.at[m], x_recv.at[m], x_ssem.at[m], x_rsem.at[m], (across, col)) for m in range(3)]
-
-    def over_chip(m):
-        c_copies[m].wait_recv()
-
-        @pl.loop(0, width // TILE)
+    first = -(-(width // TILE) // 2) * TILE
+    runs = [(m, k, pl.ds(at, size)) for m in range(3) for k, (at, size) in enumerate(((0, first), (first, width - first)))]
+    c_copies = [send(core_send.at[m, :, at], core_recv.at[m, :, at], c_ssem.at[m, k], c_rsem.at[m, k], (sib, col)) for m, k, at in runs]
+    x_copies = [send(x_send.at[m, :, at], x_recv.at[m, :, at], x_ssem.at[m, k], x_rsem.at[m, k], (across, col)) for m, k, at in runs]
+
+    def over_chip(i):
+        m, _, run = runs[i]
+        c_copies[i].wait_recv()
+
+        @pl.loop(run.start // TILE, (run.start + run.size) // TILE)
         def _(t):
             at = pl.ds(pl.multiple_of(t * TILE, TILE), TILE)
             total = own[m, :, at] + core_recv[m, :, at]
             own[m, :, at] = total
             x_send[m, :, at] = total.astype(BF16)
-        x_copies[m].start()
-
-    gather(0)
-    for m in range(3):
-        if m == 2:
-            gather(1)
-        w_copies[m].wait()
-        forward(m)
-        c_copies[m].start()
-        if m > 0:
-            over_chip(m - 1)
-    over_chip(2)
+        x_copies[i].start()
+
+    spread(0)
+    relay(0)
+    spread(1)
+    complete(0)
+    for i, (m, k, run) in enumerate(runs):
+        if k == 0:
+            if m == 2:
+                over_chip(i - 1)
+                complete(1)
+            w_copies[m].wait()
+        forward(m, run)
+        c_copies[i].start()
+        if i > 0 and not (m == 2 and k == 0):
+            over_chip(i - 1)
+        if i == RELAY:
+            relay(1)
+    over_chip(len(runs) - 1)
 
     outs = [
         pltpu.make_async_copy(src, dst, out_sem.at[k])
@@ -145,8 +160,8 @@
     outs[0].start()
     outs[1].start()
 
-    for m in range(3):
-        x_copies[m].wait_recv()
+    for copy in x_copies:
+        copy.wait_recv()
 
     @pl.loop(0, width // TILE)
     def _(t):
@@ -260,7 +275,7 @@
             pltpu.VMEM((GROUPS, 3, n, span), BF16),
             pltpu.VMEM((GROUPS, n, span), F32),
             dma((3,)), dma((5,)), dma((2, 7)), dma((2, 7)),
-            dma((3,)), dma((3,)), dma((3,)), dma((3,)),
+            dma((3, 2)), dma((3, 2)), dma((3, 2)), dma((3, 2)),
             dma((3,)), dma((3,)), dma((GROUPS,)), dma((GROUPS,)),
             dma((GROUPS, 3)), dma((GROUPS, 3)),
         ],
@@ -270,45 +285,41 @@
     )(tokens, cotangent, gate_weight, up_weight, down_weight)
 
 
-def weight_kernel(last, tok_ref, dg_ref, du_ref, hid_ref, cot_ref, gg_ref, gu_ref, gd_ref):
-    tok = tok_ref[...]
-    gg_ref[...] = contract_first(tok, dg_ref[...]).astype(BF16)
-    gu_ref[...] = contract_first(tok, du_ref[...]).astype(BF16)
-
-    @pl.when(pl.program_id(0) <= last)
+def weight_kernel(tok_ref, dg_ref, du_ref, hid_ref, cot_ref, gg_ref, gu_ref, gd_ref, turned):
+    @pl.when(pl.program_id(0) == 0)
     def _():
-        gd_ref[...] = contract_first(hid_ref[...], cot_ref[...]).astype(BF16)
+        turned[...] = tok_ref[...].T
+
+    tok = turned[...]
+    gg_ref[...] = jnp.dot(tok, dg_ref[...], preferred_element_type=F32).astype(BF16)
+    gu_ref[...] = jnp.dot(tok, du_ref[...], preferred_element_type=F32).astype(BF16)
+    gd_ref[...] = contract_first(hid_ref[...], cot_ref[...]).astype(BF16)
 
 
 def weight_grads(tok_all, dg, du, hid, cot_all):
     rows, depth = tok_all.shape
     width = dg.shape[1]
-    last = width // TILE - 1
 
     def whole(array):
         return pl.BlockSpec(array.shape, lambda i: (0, 0))
 
+    tile = pl.BlockSpec((rows, TILE), lambda i: (0, i))
     return pl.pallas_call(
-        functools.partial(weight_kernel, last),
-        grid=(depth // TILE,),
+        weight_kernel,
+        grid=(width // TILE,),
         out_shape=(
             jax.ShapeDtypeStruct((depth, width), BF16),
             jax.ShapeDtypeStruct((depth, width), BF16),
             jax.ShapeDtypeStruct((width, depth), BF16),
         ),
-        in_specs=[
-            pl.BlockSpec((rows, TILE), lambda i: (0, i)),
-            whole(dg),
-            whole(du),
-            pl.BlockSpec((rows, TILE), lambda i: (0, jnp.minimum(i, last))),
-            whole(cot_all),
-        ],
+        in_specs=[whole(tok_all), tile, tile, tile, whole(cot_all)],
         out_specs=(
-            pl.BlockSpec((TILE, width), lambda i: (i, 0)),
-            pl.BlockSpec((TILE, width), lambda i: (i, 0)),
-            pl.BlockSpec((TILE, depth), lambda i: (jnp.minimum(i, last), 0)),
-        ),
-        compiler_params=pltpu.CompilerParams(vmem_limit_bytes=40 * 1024 * 1024),
+            pl.BlockSpec((depth, TILE), lambda i: (0, i)),
+            pl.BlockSpec((depth, TILE), lambda i: (0, i)),
+            pl.BlockSpec((TILE, depth), lambda i: (i, 0)),
+        ),
+        scratch_shapes=[pltpu.VMEM((depth, rows), BF16)],
+        compiler_params=pltpu.CompilerParams(vmem_limit_bytes=62 * 1024 * 1024),
     )(tok_all, dg, du, hid, cot_all)
 
 

time: 81.8 us -> 69.3 us (0.85)
  Pallas kernels: 74.1 us -> 66.8 us
  local copies, waits for them, and re-layouts: 6.6 us -> 1.47 us
    pallas_call x1, Pallas kernels: 62.8 us -> 56 us  [main(): pl.pallas_call(main_kernel, out_shape=(jax.ShapeDtypeStruct((n, depth), B...]
    unnamed x11 -> x1, local copies, waits for them, and re-layouts: 6.6 us -> 1.47 us
where the time goes in v2:
time: 69.3 us; the launch traced here: 68.9 us
  Pallas kernels  66.8 us (96%)
  local copies, waits for them, and re-layouts  1.47 us (2%)
    pallas_call x1, Pallas kernels, main(): pl.pallas_call(main_kernel, out_shape=(jax.ShapeDtypeStruct((n, depth), B...  56 us
    pallas_call x1, Pallas kernels, weight_grads(): pl.pallas_call(weight_kernel, grid=(width // TILE,), out_shape=(jax.Shape...  10.8 us
    unnamed x1, local copies, waits for them, and re-layouts  1.47 us

profile of v2, /device:TPU:0, one launch (start us, length us, event | category | flops | bytes accessed | tf_op | source)
XLA Modules:
  0.0 68.9 jit_solution(9019142220349137423)
XLA Ops:
  0.6 56.0 %shard_map.84 = (bf16[16,2048]{1,0:T(8,128)(2,1)}, bf16[128,2048]{1,0:T(8,128)(2,1)}, bf16[128,2048]{1,0:T(8,128)(2,1)}, bf16[128,1792]{1,0:T(8,128)(2,1)}, bf16...) custom-call(bf16[16,2048]{1,0:T(8,128)(2,1)} %tok_ref.1, bf16[16,2048]{1,0:T(8,128)(2,1)} %cot_ref.1, ...), custom_call_target="tpu_custom_call" | custom-call | tf_op jit(solution)/shard_map/pallas_call | solution.py:245
  56.6 10.8 %shard_map.85 = (bf16[2048,1792]{1,0:T(8,128)(2,1)}, bf16[2048,1792]{1,0:T(8,128)(2,1)}, bf16[1792,2048]{1,0:T(8,128)(2,1)}) custom-call(bf16[128,2048]{1,0:T(8,128)(2,1)} %get-tuple-element.14.tok_ref, bf16[128,1792]{1,0:T(8,128)(2,1)} %get-tuple-element.15.dg_ref, bf16[128,1792]{1,0:T(8,128)(2,1)} %get-tuple-element.16.du_ref, ...), custom_call_target="tpu_custom_call" | custom-call | tf_op jit(solution)/shard_map/pallas_call | solution.py:307
  67.4 1.5 %copy.10 = bf16[16,2048]{1,0:T(8,128)(2,1)} copy(bf16[16,2048]{1,0:T(8,128)(2,1)} %get-tuple-element.26) | data formatting | bytes 131072
